TPU v7x, 512 devices: a whole 4x4x16 slice. The times are simulated.
512 devices in a mesh: ctx: 32 (over y, z_hi, core), fsdp: 16 (over z_lo, x).
Axes of the slice: x: 4, y: 4, z: 16 (z_hi: 4, z_lo: 4; z = z_hi * 4 + z_lo), core: 2. Of those that a mesh axis runs over, the one named last changes fastest.
Arguments:
- events: bfloat16 [8192, 4096], P('ctx'), may hold values from -6 to 6
- tile_mask: int32 [64, 2], P('ctx'), may hold values 0 or 1
- initial_state: float32 [16, 128, 128], P('fsdp'), may hold values from -96 to 96
- w_query: bfloat16 [4096, 2048], P('ctx', 'fsdp'), may hold values from -0.09375 to 0.09375
- w_key: bfloat16 [4096, 2048], P('ctx', 'fsdp'), may hold values from -0.09375 to 0.09375
- w_value: bfloat16 [4096, 2048], P('ctx', 'fsdp'), may hold values from -0.09375 to 0.09375
- cotangent: bfloat16 [8192, 2048], P('ctx', 'fsdp'), may hold values from -6 to 6
Outputs:
- attended: bfloat16 [8192, 2048], P('ctx', 'fsdp')
- events_grad: bfloat16 [8192, 4096], P('ctx')
- query_grad: bfloat16 [4096, 2048], P('ctx', 'fsdp')
- key_grad: bfloat16 [4096, 2048], P('ctx', 'fsdp')
- value_grad: bfloat16 [4096, 2048], P('ctx', 'fsdp')
Inputs may be any that keep to these rules, and one draw needn't show every extreme that they name: `tile_mask`: only entries whose column is not above the row's tile place within its block of 256 events are read.
All inputs are finite; a program needn't handle non-finite values.
Results may differ from a plain program's by a relative error of at most 0.03.
Values may be sent and summed in bfloat16 or wider, within the bound.
No kernel may reach another device: no remote copies, remote signals or barrier semaphores. Data moves between devices by JAX's collectives and lax.ppermute only.
A program may use at most 64 MiB of HBM per device.

v0:
```python
import jax
import jax.numpy as jnp
from jax import lax
from jax.sharding import PartitionSpec as P

HDIM = 128
TILE = 128
epsilon = 1e-06


def prefix(array, axis, combine, identity, reverse):
    count, index = (lax.axis_size(axis), lax.axis_index(axis))
    everything = lax.all_gather(array.astype(jnp.bfloat16), axis)
    start = jnp.broadcast_to(jnp.asarray(identity, array.dtype), array.shape)

    def turn(k, before):
        at = count - 1 - k if reverse else k
        reached = at > index if reverse else at < index
        new = combine(before, everything[at].astype(array.dtype))
        return jnp.where(reached, new, before)

    return lax.fori_loop(0, count, turn, start)


def allowed_pairs(mask_block, tile):
    count = mask_block.shape[0]
    size = count * tile
    row_index = lax.broadcasted_iota(jnp.int32, (size, size), 0)
    col_index = lax.broadcasted_iota(jnp.int32, (size, size), 1)
    tiled = jnp.repeat(jnp.repeat(mask_block, tile, axis=0), tile, axis=1)
    return jnp.where((col_index <= row_index) & (tiled > 0), 1.0, 0.0).astype(jnp.float32)


def add_states(earlier, later):
    return earlier + later


def block_prefix(local_term, reverse):
    return prefix(local_term, "ctx", add_states, jnp.zeros_like(local_term), reverse)


def on_device(events, tile_mask, initial_state, w_query, w_key, w_value, cotangent):
    event_count, head_width = cotangent.shape
    head_count = head_width // HDIM
    stacked = jnp.stack((w_query, w_key, w_value))
    allowed = allowed_pairs(tile_mask, TILE)
    panels = lax.all_gather(stacked, "ctx", axis=1, tiled=True)
    projected = jnp.einsum("td,kdw->ktw", events, panels, preferred_element_type=jnp.float32)
    projected = projected.astype(jnp.bfloat16).reshape(3, event_count, head_count, HDIM)
    queries, key_rows, value_rows = (projected[0], projected[1], projected[2])
    local_state = jnp.einsum(
        "thd,the->hde", key_rows, value_rows, preferred_element_type=jnp.float32
    )
    carried_bf = (block_prefix(local_state, False) + initial_state).astype(jnp.bfloat16)
    scores = (
        jnp.einsum("thd,shd->hts", queries, key_rows, preferred_element_type=jnp.float32)
        * allowed[None]
    )
    mixing = scores.astype(jnp.bfloat16)
    mixture = jnp.einsum("hts,shd->thd", mixing, value_rows, preferred_element_type=jnp.float32)
    mixture = mixture + jnp.einsum(
        "thd,hde->the", queries, carried_bf, preferred_element_type=jnp.float32
    )
    inverse_rms = lax.rsqrt(jnp.mean(mixture * mixture, axis=-1, keepdims=True) + epsilon)
    attended = (mixture * inverse_rms).astype(jnp.bfloat16).reshape(event_count, head_width)
    upstream = cotangent.reshape(event_count, head_count, HDIM).astype(jnp.float32)
    mixture_grad = (
        inverse_rms * upstream
        - mixture * inverse_rms**3 * jnp.mean(upstream * mixture, axis=-1, keepdims=True)
    ).astype(jnp.bfloat16)
    score_grad = (
        jnp.einsum("the,she->hts", mixture_grad, value_rows, preferred_element_type=jnp.float32)
        * allowed[None]
    ).astype(jnp.bfloat16)
    local_grad = jnp.einsum(
        "thd,the->hde", queries, mixture_grad, preferred_element_type=jnp.float32
    )
    later_bf = block_prefix(local_grad, True).astype(jnp.bfloat16)
    query_part = jnp.einsum(
        "hts,shd->thd", score_grad, key_rows, preferred_element_type=jnp.float32
    )
    query_part = query_part + jnp.einsum(
        "the,hde->thd", mixture_grad, carried_bf, preferred_element_type=jnp.float32
    )
    key_part = jnp.einsum("hts,thd->shd", score_grad, queries, preferred_element_type=jnp.float32)
    key_part = key_part + jnp.einsum(
        "she,hde->shd", value_rows, later_bf, preferred_element_type=jnp.float32
    )
    value_part = jnp.einsum(
        "hts,the->she", mixing, mixture_grad, preferred_element_type=jnp.float32
    )
    value_part = value_part + jnp.einsum(
        "shd,hde->she", key_rows, later_bf, preferred_element_type=jnp.float32
    )
    grads = (
        jnp.stack((query_part, key_part, value_part))
        .astype(jnp.bfloat16)
        .reshape(3, event_count, head_width)
    )
    partial_grad = jnp.einsum("ktw,kdw->td", grads, panels, preferred_element_type=jnp.float32)
    events_grad = lax.psum(partial_grad.astype(jnp.bfloat16), "fsdp")
    summed = lax.psum_scatter(
        jnp.einsum("td,ktw->dkw", events, grads, preferred_element_type=jnp.float32).astype(
            jnp.bfloat16
        ),
        "ctx",
        scatter_dimension=0,
        tiled=True,
    )
    return (attended, events_grad, summed[:, 0], summed[:, 1], summed[:, 2])


def solution(mesh):
    placed = (
        P("ctx", None),
        P("ctx", None),
        P("fsdp", None, None),
        P("ctx", "fsdp"),
        P("ctx", "fsdp"),
        P("ctx", "fsdp"),
        P("ctx", "fsdp"),
    )
    return jax.shard_map(
        on_device,
        mesh=mesh,
        in_specs=placed,
        out_specs=(
            P("ctx", "fsdp"),
            P("ctx", None),
            P("ctx", "fsdp"),
            P("ctx", "fsdp"),
            P("ctx", "fsdp"),
        ),
        check_vma=False,
    )
```

profile of v0, /device:TPU:8, one launch (start us, length us, event | category | flops | bytes accessed | tf_op | source)
XLA Modules:
  0.0 613.5 jit_solution(2426722656759367331)
XLA Ops:
  7.2 1.0 copy.38
  8.2 0.9 copy.39
  9.1 0.9 copy.40
  10.8 97.0 %all-gather.6.cloned.1.call-done = bf16[3,4096,128]{1,2,0:T(8,128)(2,1)} async-done(((bf16[3,128,128]{1,2,0:T(8,128)(2,1)}), bf16[3,4096,128]{1,2,0:T(8,128)(2,1)}) %all-gather.6.cloned.1.call-update) | async-done | bytes 3145744 | tf_op jit(solution)/shard_map/all_gather | solution.py:47
  107.8 2.9 fusion.9
  112.3 63.8 %all-gather.8.cloned.1.call-done = bf16[4096,128]{1,0:T(8,128)(2,1)} async-done(((bf16[128,128]{1,0:T(8,128)(2,1)}), bf16[4096,128]{1,0:T(8,128)(2,1)}) %all-gather.8.cloned.1.call-update) | async-done | bytes 1048592 | tf_op jit(solution)/shard_map/all_gather | solution.py:13
  176.0 25.8 %while.30 = (s32[]{:T(128)}, f32[1,128,128]{2,1,0:T(8,128)S(1)}, s32[]{:T(128)}, bf16[32,1,128,128]{3,2,1,0:T(8,128)(2,1)}, s32[]{:T(128)}, /*index=5*/s32[]{:T(128)}) while((s32[]{:T(128)}, f32[1,128,128]{2,1,0:T(8,128)S(1)}, s32[]{:T(128)}, bf16[32,1,128,128]{3,2,1,0:T(8,128)(2,1)}, s32[]{:T(128)}, /*index=5*/s32[]{:T(128)}) %tuple.105), condition=%wide.region_1.2_spmd.clone, body=%wide.region_0.1_spmd.clone.sunk | while | flops 65540 | bytes 163941 | solution.py:22
  176.8 0.8 add_select_fusion.4
  177.7 0.8 add_select_fusion.4
  178.5 0.8 add_select_fusion.4
  180.9 0.8 add_select_fusion.4
  184.9 0.8 add_select_fusion.4
  188.1 0.8 add_select_fusion.4
  192.2 0.8 add_select_fusion.4
  196.2 0.8 add_select_fusion.4
  200.2 0.8 add_select_fusion.4
  203.8 65.0 %all-gather.10.cloned.1.call-done = bf16[4096,128]{1,0:T(8,128)(2,1)} async-done(((bf16[128,128]{1,0:T(8,128)(2,1)}), bf16[4096,128]{1,0:T(8,128)(2,1)}) %all-gather.10.cloned.1.call-update) | async-done | bytes 1048592 | tf_op jit(solution)/shard_map/all_gather | solution.py:13
  268.8 25.9 %while.31 = (s32[]{:T(128)}, f32[1,128,128]{2,1,0:T(8,128)S(1)}, s32[]{:T(128)}, bf16[32,1,128,128]{3,2,1,0:T(8,128)(2,1)}, s32[]{:T(128)}, /*index=5*/s32[]{:T(128)}, s32[]{:T(128)}, s32[]{:T(128)}) while((s32[]{:T(128)}, f32[1,128,128]{2,1,0:T(8,128)S(1)}, s32[]{:T(128)}, bf16[32,1,128,128]{3,2,1,0:T(8,128)(2,1)}, s32[]{:T(128)}, ...), condition=%wide.region_5.6_spmd.clone, body=%wide.region_4.5_spmd.clone.sunk | while | flops 65544 | bytes 164003 | solution.py:22
  269.6 0.8 add_select_fusion.5
  273.6 0.8 add_select_fusion.5
  276.1 0.8 add_select_fusion.5
  282.5 0.8 add_select_fusion.5
  285.0 0.8 add_select_fusion.5
  289.0 0.8 add_select_fusion.5
  291.5 0.8 add_select_fusion.5
  295.4 2.7 convolution_convert_fusion
  298.1 4.7 copy.56
  302.8 4.5 fusion
  308.1 118.9 %reduce-scatter.4.cloned.1.call-done = bf16[128,384]{1,0:T(8,128)(2,1)} async-done(((bf16[4096,384]{1,0:T(8,128)(2,1)}), bf16[128,384]{1,0:T(8,128)(2,1)}) %reduce-scatter.4.cloned.1.call-update) | async-done | bytes 98320
  427.0 1.0 copy.57
  430.2 173.7 %all-reduce.2.cloned.1.call-done = bf16[256,4096]{1,0:T(8,128)(2,1)} async-done(((bf16[256,4096]{1,0:T(8,128)(2,1)}), bf16[256,4096]{1,0:T(8,128)(2,1)}) %all-reduce.2.cloned.1.call-update) | async-done | bytes 2097168 | tf_op jit(solution)/shard_map/psum | solution.py:101
  603.8 3.1 copy.76
  (96 shorter events, 45.5 us)
Async XLA Ops:
  7.2 100.6 %copy-start = (bf16[256,4096]{1,0:T(8,128)(2,1)S(1)}, bf16[256,4096]{1,0:T(8,128)(2,1)}, u32[]{:S(2)}) copy-start(bf16[256,4096]{1,0:T(8,128)(2,1)} %param.11) | copy-start | bytes 6291460
  7.2 100.6 %all-gather.6.cloned.1.call-start = ((), (), s32[]{:S(2)}) async-start(), calls=%async_computation.1 | async-start | bytes 3244032 | tf_op jit(solution)/shard_map/all_gather | solution.py:47
  10.7 100.9 %copy-start.3 = (s32[2,2]{1,0:T(2,128)S(1)}, s32[2,2]{1,0:T(2,128)}, u32[]{:S(2)}) copy-start(s32[2,2]{1,0:T(2,128)} %param.12) | copy-start | bytes 52
  10.7 101.2 %copy-start.1 = (bf16[256,128]{1,0:T(8,128)(2,1)S(1)}, bf16[256,128]{1,0:T(8,128)(2,1)}, u32[]{:S(2)}) copy-start(bf16[256,128]{1,0:T(8,128)(2,1)} %param.17) | copy-start | bytes 196612
  10.7 191.1 %copy-start.2 = (f32[1,128,128]{2,1,0:T(8,128)S(1)}, f32[1,128,128]{2,1,0:T(8,128)}, u32[]{:S(2)}) copy-start(f32[1,128,128]{2,1,0:T(8,128)} %param.13) | copy-start | bytes 196612
  10.7 165.3 %all-gather.8.cloned.1.call-start = ((), (), s32[]{:S(2)}) async-start(), calls=%async_computation.3 | async-start | bytes 1081344 | tf_op jit(solution)/shard_map/all_gather | solution.py:13
  111.5 157.3 %all-gather.10.cloned.1.call-start = ((), (), s32[]{:S(2)}) async-start(), calls=%async_computation.4 | async-start | bytes 1081344 | tf_op jit(solution)/shard_map/all_gather | solution.py:13
  203.2 223.8 %reduce-scatter.4.cloned.1.call-start = ((), (), s32[]{:S(2)}) async-start(), calls=%async_computation.5 | async-start | bytes 3244032
  302.8 301.1 %all-reduce.2.cloned.1.call-start = ((), (), s32[]{:S(2)}) async-start(), calls=%async_computation.2 | async-start | bytes 4194304 | tf_op jit(solution)/shard_map/psum | solution.py:101
Sparse Core Ops, SparseCore 0:
  11.6 96.0 all-gather.5
  111.6 64.4 all-gather.7
  203.3 65.4 all-gather.9
  302.9 124.0 reduce-scatter.3
  430.6 173.1 all-reduce.1
where the time goes:
time: 618 us; the launch traced here: 613 us
  waiting for transfers between devices  518 us (84%)
  other arithmetic  50.9 us (8%)
  local copies, waits for them, and re-layouts  14.9 us (2%)
  between operations  14 us (2%)
  matrix products  13.5 us (2%)
    psum x1, waiting for transfers between devices, on_device(): events_grad = lax.psum(partial_grad.astype(jnp.bfloat16), 'fsdp')  174 us
    all_gather x2, waiting for transfers between devices, prefix(): everything = lax.all_gather(array.astype(jnp.bfloat16), axis)  129 us
    unnamed x6, waiting for transfers between devices  119 us
    all_gather x1, waiting for transfers between devices, on_device(): panels = lax.all_gather(stacked, 'ctx', axis=1, tiled=True)  97 us
    select_n x64, other arithmetic, turn(): return jnp.where(reached, new, before)  50.1 us
    unnamed x21, local copies, waits for them, and re-layouts  14.7 us
  transfers between devices with their start and end apart: 5, of which 5 were waited for; matrix products, arithmetic and copies ran while one was open for 2% of the time, Pallas kernels for 0%

commit v1 on v0

--- a/solution.py
+++ b/solution.py
@@ -2,6 +2,7 @@
 import jax.numpy as jnp
 from jax import lax
 from jax.sharding import PartitionSpec as P
+from jax.lax import all_gather
 
 HDIM = 128
 TILE = 128
@@ -98,7 +99,8 @@
         .reshape(3, event_count, head_width)
     )
     partial_grad = jnp.einsum("ktw,kdw->td", grads, panels, preferred_element_type=jnp.float32)
-    events_grad = lax.psum(partial_grad.astype(jnp.bfloat16), "fsdp")
+    row_data = partial_grad.astype(jnp.bfloat16)
+    events_grad = jnp.sum(all_gather(row_data, "fsdp"), axis=0)
     summed = lax.psum_scatter(
         jnp.einsum("td,ktw->dkw", events, grads, preferred_element_type=jnp.float32).astype(
             jnp.bfloat16

time: 618 us -> 811 us (1.31)
  the two profiles are of different devices: /device:TPU:8 before, /device:TPU:1 now
where the time goes in v1:
time: 811 us; the launch traced here: 806 us
  waiting for transfers between devices  701 us (86%)
  other arithmetic  63.8 us (8%)
  between operations  14 us (2%)
  matrix products  13.5 us (2%)
  local copies, waits for them, and re-layouts  11.8 us (1%)
    all_gather x1, waiting for transfers between devices, on_device(): events_grad = jnp.sum(all_gather(row_data, 'fsdp'), axis=0)  355 us
    all_gather x2, waiting for transfers between devices, prefix(): everything = lax.all_gather(array.astype(jnp.bfloat16), axis)  130 us
    unnamed x6, waiting for transfers between devices  117 us
    all_gather x1, waiting for transfers between devices, on_device(): panels = lax.all_gather(stacked, 'ctx', axis=1, tiled=True)  98.5 us
    select_n x64, other arithmetic, turn(): return jnp.where(reached, new, before)  50.1 us
  transfers between devices with their start and end apart: 5, of which 5 were waited for; matrix products, arithmetic and copies ran while one was open for 1% of the time, Pallas kernels for 0%

profile of v1, /device:TPU:1, one launch (start us, length us, event | category | flops | bytes accessed | tf_op | source)
XLA Modules:
  0.0 805.9 jit_solution(11901567820254151501)
XLA Ops:
  7.2 1.0 copy.38
  8.2 0.9 copy.39
  9.1 0.9 copy.40
  10.8 98.5 %all-gather.8.cloned.1.call-done = bf16[3,4096,128]{1,2,0:T(8,128)(2,1)} async-done(((bf16[3,128,128]{1,2,0:T(8,128)(2,1)}), bf16[3,4096,128]{1,2,0:T(8,128)(2,1)}) %all-gather.8.cloned.1.call-update) | async-done | bytes 3145744 | tf_op jit(solution)/shard_map/all_gather | solution.py:48
  109.3 2.9 fusion.9
  112.2 0.8 convolution_convert_fusion.2
  113.8 64.9 %all-gather.10.cloned.1.call-done = bf16[4096,128]{1,0:T(8,128)(2,1)} async-done(((bf16[128,128]{1,0:T(8,128)(2,1)}), bf16[4096,128]{1,0:T(8,128)(2,1)}) %all-gather.10.cloned.1.call-update) | async-done | bytes 1048592 | tf_op jit(solution)/shard_map/all_gather | solution.py:14
  178.7 25.8 %while.30 = (s32[]{:T(128)}, f32[1,128,128]{2,1,0:T(8,128)S(1)}, s32[]{:T(128)}, bf16[32,1,128,128]{3,2,1,0:T(8,128)(2,1)}, s32[]{:T(128)}, /*index=5*/s32[]{:T(128)}) while((s32[]{:T(128)}, f32[1,128,128]{2,1,0:T(8,128)S(1)}, s32[]{:T(128)}, bf16[32,1,128,128]{3,2,1,0:T(8,128)(2,1)}, s32[]{:T(128)}, /*index=5*/s32[]{:T(128)}) %tuple.104), condition=%wide.region_1.2_spmd.clone, body=%wide.region_0.1_spmd.clone.sunk | while | flops 65540 | bytes 163933 | solution.py:23
  179.5 0.8 add_select_fusion.4
  180.3 0.8 add_select_fusion.4
  182.8 0.8 add_select_fusion.4
  186.0 0.8 add_select_fusion.4
  190.0 0.8 add_select_fusion.4
  194.0 0.8 add_select_fusion.4
  198.1 0.8 add_select_fusion.4
  201.3 0.8 add_select_fusion.4
  206.5 65.0 %all-gather.12.cloned.1.call-done = bf16[4096,128]{1,0:T(8,128)(2,1)} async-done(((bf16[128,128]{1,0:T(8,128)(2,1)}), bf16[4096,128]{1,0:T(8,128)(2,1)}) %all-gather.12.cloned.1.call-update) | async-done | bytes 1048592 | tf_op jit(solution)/shard_map/all_gather | solution.py:14
  271.5 26.0 %while.31 = (s32[]{:T(128)}, f32[1,128,128]{2,1,0:T(8,128)S(1)}, s32[]{:T(128)}, bf16[32,1,128,128]{3,2,1,0:T(8,128)(2,1)}, s32[]{:T(128)}, /*index=5*/s32[]{:T(128)}, s32[]{:T(128)}, s32[]{:T(128)}) while((s32[]{:T(128)}, f32[1,128,128]{2,1,0:T(8,128)S(1)}, s32[]{:T(128)}, bf16[32,1,128,128]{3,2,1,0:T(8,128)(2,1)}, s32[]{:T(128)}, ...), condition=%wide.region_5.6_spmd.clone, body=%wide.region_4.5_spmd.clone.sunk | while | flops 65544 | bytes 163995 | solution.py:23
  275.5 0.8 add_select_fusion.5
  277.1 0.8 add_select_fusion.5
  281.2 0.8 add_select_fusion.5
  286.9 0.8 add_select_fusion.5
  291.0 0.8 add_select_fusion.5
  292.6 0.8 add_select_fusion.5
  296.6 0.8 add_select_fusion.5
  298.1 2.7 convolution_convert_fusion
  300.8 4.6 copy.56
  305.5 4.5 fusion
  310.7 117.2 %reduce-scatter.4.cloned.1.call-done = bf16[128,384]{1,0:T(8,128)(2,1)} async-done(((bf16[4096,384]{1,0:T(8,128)(2,1)}), bf16[128,384]{1,0:T(8,128)(2,1)}) %reduce-scatter.4.cloned.1.call-update) | async-done | bytes 98320
  428.0 1.0 copy.57
  431.2 355.2 %all-gather.14.cloned.1.call-done = bf16[4096,4096]{1,0:T(8,128)(2,1)} async-done(((bf16[256,4096]{1,0:T(8,128)(2,1)}), bf16[4096,4096]{1,0:T(8,128)(2,1)}) %all-gather.14.cloned.1.call-update) | async-done | bytes 33554448 | tf_op jit(solution)/shard_map/all_gather | solution.py:103
  786.4 13.0 %reduce_sum.32 = bf16[256,4096]{1,0:T(8,128)(2,1)} reduce(bf16[16,256,4096]{2,1,0:T(8,128)(2,1)} %bitcast.133, bf16[]{:T(256)} %constant.85.clone.1), dimensions={0}, to_apply=%region_6.7 | reduce | flops 15728640 | bytes 35651584 | tf_op jit(solution)/shard_map/reduce_sum | solution.py:103
  (96 shorter events, 45.4 us)
Async XLA Ops:
  7.2 102.1 %copy-start = (bf16[256,4096]{1,0:T(8,128)(2,1)S(1)}, bf16[256,4096]{1,0:T(8,128)(2,1)}, u32[]{:S(2)}) copy-start(bf16[256,4096]{1,0:T(8,128)(2,1)} %param.11) | copy-start | bytes 6291460
  7.2 102.1 %all-gather.8.cloned.1.call-start = ((), (), s32[]{:S(2)}) async-start(), calls=%async_computation.1 | async-start | bytes 3244032 | tf_op jit(solution)/shard_map/all_gather | solution.py:48
  10.7 102.4 %copy-start.3 = (s32[2,2]{1,0:T(2,128)S(1)}, s32[2,2]{1,0:T(2,128)}, u32[]{:S(2)}) copy-start(s32[2,2]{1,0:T(2,128)} %param.12) | copy-start | bytes 52
  10.7 102.8 %copy-start.1 = (bf16[256,128]{1,0:T(8,128)(2,1)S(1)}, bf16[256,128]{1,0:T(8,128)(2,1)}, u32[]{:S(2)}) copy-start(bf16[256,128]{1,0:T(8,128)(2,1)} %param.17) | copy-start | bytes 196612
  10.7 193.8 %copy-start.2 = (f32[1,128,128]{2,1,0:T(8,128)S(1)}, f32[1,128,128]{2,1,0:T(8,128)}, u32[]{:S(2)}) copy-start(f32[1,128,128]{2,1,0:T(8,128)} %param.13) | copy-start | bytes 196612
  10.7 168.0 %all-gather.10.cloned.1.call-start = ((), (), s32[]{:S(2)}) async-start(), calls=%async_computation.2 | async-start | bytes 1081344 | tf_op jit(solution)/shard_map/all_gather | solution.py:14
  113.0 158.4 %all-gather.12.cloned.1.call-start = ((), (), s32[]{:S(2)}) async-start(), calls=%async_computation.3 | async-start | bytes 1081344 | tf_op jit(solution)/shard_map/all_gather | solution.py:14
  205.8 222.1 %reduce-scatter.4.cloned.1.call-start = ((), (), s32[]{:S(2)}) async-start(), calls=%async_computation.5 | async-start | bytes 3244032
  305.4 481.0 %all-gather.14.cloned.1.call-start = ((), (), s32[]{:S(2)}) async-start(), calls=%async_computation.4 | async-start | bytes 35651584 | tf_op jit(solution)/shard_map/all_gather | solution.py:103
Sparse Core Ops, SparseCore 0:
  11.6 97.6 all-gather.7
  113.1 65.5 all-gather.9
  206.0 65.4 all-gather.11
  305.5 122.3 reduce-scatter.3
  430.7 355.6 all-gather.13

commit v2 on v0

--- a/solution.py
+++ b/solution.py
@@ -44,7 +44,10 @@
     head_count = head_width // HDIM
     stacked = jnp.stack((w_query, w_key, w_value))
     allowed = allowed_pairs(tile_mask, TILE)
-    panels = lax.all_gather(stacked, "ctx", axis=1, tiled=True)
+    devices = lax.axis_size("ctx")
+    blocks = jnp.stack([stacked for _ in range(devices)])
+    blocks = lax.all_to_all(blocks, "ctx", split_axis=0, concat_axis=0)
+    panels = jnp.concatenate(blocks, axis=1)
     projected = jnp.einsum("td,kdw->ktw", events, panels, preferred_element_type=jnp.float32)
     projected = projected.astype(jnp.bfloat16).reshape(3, event_count, head_count, HDIM)
     queries, key_rows, value_rows = (projected[0], projected[1], projected[2])

time: 618 us -> 680 us (1.10)
  blocking collectives: 0 us -> 159 us
  waiting for transfers between devices: 518 us -> 424 us
    all_to_all x0 -> x1, blocking collectives: none -> 159 us  [on_device(): blocks = lax.all_to_all(blocks, 'ctx', split_axis=0, concat_axis=0)]
    all_gather x1 -> x0, waiting for transfers between devices: 97 us -> none  [on_device(): panels = lax.all_gather(stacked, 'ctx', axis=1, tiled=True)]
    unnamed x21 -> x20, local copies, waits for them, and re-layouts: 14.7 us -> 12.5 us
    unnamed x6 -> x5, waiting for transfers between devices: 119 us -> 119 us
  transfers between devices with their start and end apart: 5 -> 4, of which waited for: 5 -> 4; matrix products, arithmetic and copies ran while one was open for 2% -> 1% of each run, Pallas kernels for 0% -> 0%
where the time goes in v2:
time: 680 us; the launch traced here: 675 us
  waiting for transfers between devices  424 us (62%)
  blocking collectives  159 us (23%)
  other arithmetic  51.2 us (8%)
  between operations  14 us (2%)
  local copies, waits for them, and re-layouts  13.7 us (2%)
  matrix products  11.6 us (2%)
    psum x1, waiting for transfers between devices, on_device(): events_grad = lax.psum(partial_grad.astype(jnp.bfloat16), 'fsdp')  174 us
    all_to_all x1, blocking collectives, on_device(): blocks = lax.all_to_all(blocks, 'ctx', split_axis=0, concat_axis=0)  159 us
    all_gather x2, waiting for transfers between devices, prefix(): everything = lax.all_gather(array.astype(jnp.bfloat16), axis)  131 us
    unnamed x5, waiting for transfers between devices  119 us
    select_n x64, other arithmetic, turn(): return jnp.where(reached, new, before)  50.1 us
  transfers between devices with their start and end apart: 4, of which 4 were waited for; matrix products, arithmetic and copies ran while one was open for 1% of the time, Pallas kernels for 0%

profile of v2, /device:TPU:8, one launch (start us, length us, event | category | flops | bytes accessed | tf_op | source)
XLA Modules:
  0.0 675.1 jit_solution(5536399203788660780)
XLA Ops:
  7.2 0.9 pad_maximum_fusion.1
  9.1 158.9 %all_to_all.5 = bf16[32,3,128,128]{2,3,1,0:T(8,128)(2,1)S(1)} all-to-all(bf16[32,3,128,128]{2,3,1,0:T(8,128)(2,1)S(1)} %stack.22), channel_id=1, replica_groups=mesh['ctx'=32,'fsdp'=16] {'ctx'}, dimensions={0} | all-to-all | bytes 6291456 | tf_op jit(solution)/shard_map/all_to_all | solution.py:49
  168.0 1.0 fusion.15
  171.2 66.4 %all-gather.5.cloned.1.call-done = bf16[4096,128]{1,0:T(8,128)(2,1)} async-done(((bf16[128,128]{1,0:T(8,128)(2,1)}), bf16[4096,128]{1,0:T(8,128)(2,1)}) %all-gather.5.cloned.1.call-update) | async-done | bytes 1048592 | tf_op jit(solution)/shard_map/all_gather | solution.py:13
  237.6 25.8 %while.30 = (s32[]{:T(128)}, f32[1,128,128]{2,1,0:T(8,128)S(1)}, s32[]{:T(128)}, bf16[32,1,128,128]{3,2,1,0:T(8,128)(2,1)}, s32[]{:T(128)}, /*index=5*/s32[]{:T(128)}) while((s32[]{:T(128)}, f32[1,128,128]{2,1,0:T(8,128)S(1)}, s32[]{:T(128)}, bf16[32,1,128,128]{3,2,1,0:T(8,128)(2,1)}, s32[]{:T(128)}, /*index=5*/s32[]{:T(128)}) %tuple.103), condition=%wide.region_1.2_spmd.clone, body=%wide.region_0.1_spmd.clone.sunk | while | flops 65540 | bytes 163941 | solution.py:22
  238.4 0.8 add_select_fusion.4
  239.2 0.8 add_select_fusion.4
  240.0 0.8 add_select_fusion.4
  240.8 0.8 add_select_fusion.4
  241.6 0.8 add_select_fusion.4
  242.4 0.8 add_select_fusion.4
  243.2 0.8 add_select_fusion.4
  245.6 0.8 add_select_fusion.4
  249.7 0.8 add_select_fusion.4
  252.9 0.8 add_select_fusion.4
  256.9 0.8 add_select_fusion.4
  261.0 0.8 add_select_fusion.4
  265.3 65.0 %all-gather.7.cloned.1.call-done = bf16[4096,128]{1,0:T(8,128)(2,1)} async-done(((bf16[128,128]{1,0:T(8,128)(2,1)}), bf16[4096,128]{1,0:T(8,128)(2,1)}) %all-gather.7.cloned.1.call-update) | async-done | bytes 1048592 | tf_op jit(solution)/shard_map/all_gather | solution.py:13
  330.3 25.9 %while.31 = (s32[]{:T(128)}, f32[1,128,128]{2,1,0:T(8,128)S(1)}, s32[]{:T(128)}, bf16[32,1,128,128]{3,2,1,0:T(8,128)(2,1)}, s32[]{:T(128)}, /*index=5*/s32[]{:T(128)}, s32[]{:T(128)}, s32[]{:T(128)}) while((s32[]{:T(128)}, f32[1,128,128]{2,1,0:T(8,128)S(1)}, s32[]{:T(128)}, bf16[32,1,128,128]{3,2,1,0:T(8,128)(2,1)}, s32[]{:T(128)}, ...), condition=%wide.region_5.6_spmd.clone, body=%wide.region_4.5_spmd.clone.sunk | while | flops 65544 | bytes 164003 | solution.py:22
  334.4 0.8 add_select_fusion.5
  336.8 0.8 add_select_fusion.5
  343.3 0.8 add_select_fusion.5
  345.7 0.8 add_select_fusion.5
  349.8 0.8 add_select_fusion.5
  352.2 0.8 add_select_fusion.5
  356.9 2.7 convolution_convert_fusion
  359.6 4.7 copy.51
  364.4 4.5 fusion
  369.6 118.9 %reduce-scatter.4.cloned.1.call-done = bf16[128,384]{1,0:T(8,128)(2,1)} async-done(((bf16[4096,384]{1,0:T(8,128)(2,1)}), bf16[128,384]{1,0:T(8,128)(2,1)}) %reduce-scatter.4.cloned.1.call-update) | async-done | bytes 98320
  488.5 1.0 copy.52
  491.7 173.8 %all-reduce.2.cloned.1.call-done = bf16[256,4096]{1,0:T(8,128)(2,1)} async-done(((bf16[256,4096]{1,0:T(8,128)(2,1)}), bf16[256,4096]{1,0:T(8,128)(2,1)}) %all-reduce.2.cloned.1.call-update) | async-done | bytes 2097168 | tf_op jit(solution)/shard_map/psum | solution.py:104
  665.5 3.1 copy.84
  (95 shorter events, 44.6 us)
Async XLA Ops:
  7.2 160.8 %copy-start = (bf16[256,4096]{1,0:T(8,128)(2,1)S(1)}, bf16[256,4096]{1,0:T(8,128)(2,1)}, u32[]{:S(2)}) copy-start(bf16[256,4096]{1,0:T(8,128)(2,1)} %param.11) | copy-start | bytes 6291460
  7.2 230.4 %all-gather.5.cloned.1.call-start = ((), (), s32[]{:S(2)}) async-start(), calls=%async_computation.3 | async-start | bytes 1081344 | tf_op jit(solution)/shard_map/all_gather | solution.py:13
  168.0 1.6 copy-start.1
  168.0 2.5 copy-start.4
  168.0 2.9 copy-start.2
  168.0 95.4 %copy-start.3 = (f32[1,128,128]{2,1,0:T(8,128)S(1)}, f32[1,128,128]{2,1,0:T(8,128)}, u32[]{:S(2)}) copy-start(f32[1,128,128]{2,1,0:T(8,128)} %param.13) | copy-start | bytes 196612
  170.4 159.9 %all-gather.7.cloned.1.call-start = ((), (), s32[]{:S(2)}) async-start(), calls=%async_computation.4 | async-start | bytes 1081344 | tf_op jit(solution)/shard_map/all_gather | solution.py:13
  264.7 223.8 %reduce-scatter.4.cloned.1.call-start = ((), (), s32[]{:S(2)}) async-start(), calls=%async_computation.5 | async-start | bytes 3244032
  364.3 301.1 %all-reduce.2.cloned.1.call-start = ((), (), s32[]{:S(2)}) async-start(), calls=%async_computation.2 | async-start | bytes 4194304 | tf_op jit(solution)/shard_map/psum | solution.py:104
Sparse Core Ops, SparseCore 0:
  170.5 67.0 all-gather.4
  264.8 65.4 all-gather.6
  364.4 124.0 reduce-scatter.3
  492.1 173.2 all-reduce.1
